TPU v7x, 256 devices: a whole 4x4x8 slice. The times are simulated.
256 devices in a mesh: seq: 32 (over y, x, core), dp: 8 (over z).
Axes of the slice: x: 4, y: 4, z: 8, core: 2. Of those that a mesh axis runs over, the one named last changes fastest.
Arguments:
- cross_queries: bfloat16 [8, 4096, 4096], P('dp', 'seq')
- cross_cotangent: bfloat16 [8, 4096, 4096], P('dp', 'seq'), may hold values from -6 to 6
- gate: float32 [32], replicated, may hold values from -1.5 to 1.5
- vision_kv: bfloat16 [8, 32, 1601, 1024], P('dp', 'seq')
- block_map: int32 [8, 32], P('dp', 'seq'), may hold values from 0 to 2, as said below
- self_queries: bfloat16 [8, 4096, 4096], P('dp', 'seq')
- self_keys: bfloat16 [8, 4096, 512], P('dp', 'seq')
- self_values: bfloat16 [8, 4096, 512], P('dp', 'seq'), may hold values from -6 to 6
- self_cotangent: bfloat16 [8, 4096, 4096], P('dp', 'seq'), may hold values from -6 to 6
- doc_ids: int32 [8, 4096], P('dp', 'seq'), may hold values from 0 to 15, never falling along the last dimension, each value on 1 to 512 neighbouring positions
Outputs:
- cross_query_grad: bfloat16 [8, 4096, 4096], P('dp', 'seq')
- gate_grad: float32 [32], replicated
- vision_grad: bfloat16 [8, 32, 1601, 1024], P('dp', 'seq')
- self_query_grad: bfloat16 [8, 4096, 4096], P('dp', 'seq')
- self_key_grad: bfloat16 [8, 4096, 512], P('dp', 'seq')
- self_value_grad: bfloat16 [8, 4096, 512], P('dp', 'seq')
Inputs may be any that keep to these rules, and one draw needn't show every extreme that they name: `block_map`: 0: the span attends its own image block; 1: the block before it; 2: no image. The first span of a sequence never holds 1. `doc_ids`: ids never fall along a sequence; each document holds at most 512 tokens.
All inputs are finite; a program needn't handle non-finite values.
Results may differ from a plain program's by a relative error of at most 0.012.
The roundings to bfloat16 on the way count: a program that leaves them out, or rounds other values in their place, can miss the bound.
Values may be sent and summed in bfloat16 or wider, within the bound.
A program may use at most 128 MiB of HBM per device.

v0:
```python
import jax
import jax.numpy as jnp
from jax import lax
from jax.sharding import PartitionSpec as P

HEADS = 32
KVH = 4
HD = 128
VROWS = 1601
QBLOCK = 256
MOST = 512


NEG_LARGE = -1e30


def passed_along(value, axis, steps):
    count = lax.axis_size(axis)
    first, last = (max(0, -steps), min(count, count - steps))
    return lax.ppermute(value, axis, [(source, source + steps) for source in range(first, last)])


def cross_span(queries, cotangent, block, gate):
    rows = queries.shape[0]
    group_size = HEADS // KVH
    factor = HD ** (-0.5)
    tanh_gate = jnp.tanh(gate)
    query_heads = queries.reshape(rows, KVH, group_size, HD).transpose(1, 0, 2, 3)
    cot_heads = cotangent.reshape(rows, KVH, group_size, HD).transpose(1, 0, 2, 3)
    key_heads = block[:, : KVH * HD].reshape(VROWS, KVH, HD).transpose(1, 0, 2)
    value_heads = block[:, KVH * HD :].reshape(VROWS, KVH, HD).transpose(1, 0, 2)
    gate_heads = tanh_gate.reshape(KVH, group_size)

    def one_head(operands):
        query_one, cot_one, key_one, value_one, gate_one = operands
        scores = (
            jnp.einsum("rgd,vd->rgv", query_one, key_one, preferred_element_type=jnp.float32)
            * factor
        )
        row_max = jnp.max(scores, axis=-1, keepdims=True)
        weights = jnp.exp(scores - row_max)
        weights = weights / jnp.sum(weights, axis=-1, keepdims=True)
        weights_low = weights.astype(jnp.bfloat16)
        attended = jnp.einsum(
            "rgv,vd->rgd", weights_low, value_one, preferred_element_type=jnp.float32
        )
        cot_wide = cot_one.astype(jnp.float32)
        inner = jnp.sum(cot_wide * attended, axis=-1)
        out_grad = (gate_one[None, :, None] * cot_wide).astype(jnp.bfloat16)
        delta = gate_one[None, :] * inner
        weight_grad = jnp.einsum(
            "rgd,vd->rgv", out_grad, value_one, preferred_element_type=jnp.float32
        )
        score_grad = (weights * (weight_grad - delta[:, :, None])).astype(jnp.bfloat16)
        query_grad = (
            jnp.einsum("rgv,vd->rgd", score_grad, key_one, preferred_element_type=jnp.float32)
            * factor
        )
        key_grad = (
            jnp.einsum("rgv,rgd->vd", score_grad, query_one, preferred_element_type=jnp.float32)
            * factor
        )
        value_grad = jnp.einsum(
            "rgv,rgd->vd", weights_low, out_grad, preferred_element_type=jnp.float32
        )
        return (query_grad, key_grad, value_grad, jnp.sum(inner, axis=0))

    query_grad, key_grad, value_grad, inner_sum = lax.map(
        one_head, (query_heads, cot_heads, key_heads, value_heads, gate_heads)
    )
    query_grad = query_grad.transpose(1, 0, 2, 3).reshape(rows, HEADS * HD).astype(jnp.bfloat16)
    block_grad = jnp.concatenate(
        [
            key_grad.transpose(1, 0, 2).reshape(VROWS, KVH * HD),
            value_grad.transpose(1, 0, 2).reshape(VROWS, KVH * HD),
        ],
        axis=1,
    )
    gate_term = (1.0 - tanh_gate * tanh_gate) * inner_sum.reshape(HEADS)
    return (query_grad, block_grad, gate_term)


def self_attend(query_heads, key_heads, value_heads, cot_heads, docs):
    all_tokens = query_heads.shape[0]
    factor = HD ** (-0.5)
    window = QBLOCK + MOST
    query_pos = jnp.arange(QBLOCK, dtype=jnp.int32)
    key_pos = jnp.arange(window, dtype=jnp.int32)

    def step(totals, block_index):
        key_total, value_total = totals
        first_row = block_index * QBLOCK
        key_start = jnp.maximum(first_row - MOST, 0)
        query_block = lax.dynamic_slice_in_dim(query_heads, first_row, QBLOCK, 0)
        cot_block = lax.dynamic_slice_in_dim(cot_heads, first_row, QBLOCK, 0)
        key_window = lax.dynamic_slice_in_dim(key_heads, key_start, window, 0)
        value_window = lax.dynamic_slice_in_dim(value_heads, key_start, window, 0)
        query_docs = lax.dynamic_slice_in_dim(docs, first_row, QBLOCK, 0)
        key_docs = lax.dynamic_slice_in_dim(docs, key_start, window, 0)
        allowed = ((key_start + key_pos)[None, :] <= (first_row + query_pos)[:, None]) & (
            key_docs[None, :] == query_docs[:, None]
        )
        scores = (
            jnp.einsum("qhd,khd->hqk", query_block, key_window, preferred_element_type=jnp.float32)
            * factor
        )
        scores = jnp.where(allowed[None], scores, NEG_LARGE)
        row_max = jnp.max(scores, axis=-1, keepdims=True)
        weights = jnp.exp(scores - row_max)
        weights = weights / jnp.sum(weights, axis=-1, keepdims=True)
        weights_low = weights.astype(jnp.bfloat16)
        attended = jnp.einsum(
            "hqk,khd->qhd", weights_low, value_window, preferred_element_type=jnp.float32
        )
        delta = jnp.sum(cot_block.astype(jnp.float32) * attended, axis=-1)
        weight_grad = jnp.einsum(
            "qhd,khd->hqk", cot_block, value_window, preferred_element_type=jnp.float32
        )
        score_grad = (weights * (weight_grad - delta.T[:, :, None])).astype(jnp.bfloat16)
        query_grad = (
            jnp.einsum("hqk,khd->qhd", score_grad, key_window, preferred_element_type=jnp.float32)
            * factor
        ).astype(jnp.bfloat16)
        key_grad = (
            jnp.einsum("hqk,qhd->khd", score_grad, query_block, preferred_element_type=jnp.float32)
            * factor
        )
        value_grad = jnp.einsum(
            "hqk,qhd->khd", weights_low, cot_block, preferred_element_type=jnp.float32
        )
        key_total = lax.dynamic_update_slice_in_dim(
            key_total,
            lax.dynamic_slice_in_dim(key_total, key_start, window, 0) + key_grad,
            key_start,
            0,
        )
        value_total = lax.dynamic_update_slice_in_dim(
            value_total,
            lax.dynamic_slice_in_dim(value_total, key_start, window, 0) + value_grad,
            key_start,
            0,
        )
        return ((key_total, value_total), query_grad)

    zeros_grad = jnp.zeros(query_heads.shape, jnp.float32)
    block_count = all_tokens // QBLOCK
    (key_total, value_total), query_grad = lax.scan(
        step, (zeros_grad, zeros_grad), jnp.arange(block_count, dtype=jnp.int32)
    )
    return (query_grad.reshape(query_heads.shape), key_total, value_total)


def local(
    cross_queries,
    cross_cotangent,
    gate,
    vision_kv,
    block_map,
    self_queries,
    self_keys,
    self_values,
    self_cotangent,
    doc_ids,
):
    devices = lax.axis_size("seq")
    span_queries = cross_queries[0]
    span_cot = cross_cotangent[0]
    own_block = vision_kv[0, 0]
    token_rows = span_queries.shape[0]
    mine = block_map[0, 0]
    prior_block = passed_along(own_block, "seq", 1)
    picked = jnp.where(mine == 1, prior_block, own_block)
    query_grad, block_term, gate_term = cross_span(span_queries, span_cot, picked, gate)
    is_live = mine != 2
    cross_grad = jnp.where(is_live, query_grad, jnp.zeros_like(query_grad))
    gate_term = jnp.where(is_live, gate_term, jnp.zeros_like(gate_term))
    to_prior = jnp.where(mine == 1, block_term, jnp.zeros_like(block_term))
    arrived = passed_along(to_prior.astype(jnp.bfloat16), "seq", -1).astype(to_prior.dtype)
    own_term = jnp.where(mine == 0, block_term, jnp.zeros_like(block_term))
    block_grad = (own_term + arrived).astype(jnp.bfloat16)
    group_size = HEADS // KVH
    kv_width = KVH * HD
    docs = lax.all_gather(doc_ids[0], "seq", axis=0, tiled=True)
    key_rows = self_keys[0].reshape(token_rows, KVH, 1, HD)
    value_rows = self_values[0].reshape(token_rows, KVH, 1, HD)
    key_repeat = jnp.broadcast_to(key_rows, (token_rows, KVH, group_size, HD)).reshape(
        token_rows, HEADS * HD
    )
    value_repeat = jnp.broadcast_to(value_rows, (token_rows, KVH, group_size, HD)).reshape(
        token_rows, HEADS * HD
    )
    head_query, head_key, head_value, head_cot = (
        lax.all_to_all(self_queries[0], "seq", split_axis=1, concat_axis=0, tiled=True),
        lax.all_to_all(key_repeat, "seq", split_axis=1, concat_axis=0, tiled=True),
        lax.all_to_all(value_repeat, "seq", split_axis=1, concat_axis=0, tiled=True),
        lax.all_to_all(self_cotangent[0], "seq", split_axis=1, concat_axis=0, tiled=True),
    )
    all_tokens = token_rows * devices
    local_heads = HEADS // devices
    head_shape = (all_tokens, local_heads, HD)
    query_grad, key_grad, value_grad = self_attend(
        head_query.reshape(head_shape),
        head_key.reshape(head_shape),
        head_value.reshape(head_shape),
        head_cot.reshape(head_shape),
        docs,
    )
    self_grad = lax.all_to_all(
        query_grad.reshape(all_tokens, local_heads * HD),
        "seq",
        split_axis=0,
        concat_axis=1,
        tiled=True,
    )
    key_home, value_home = (
        lax.all_to_all(
            key_grad.reshape(all_tokens, local_heads * HD),
            "seq",
            split_axis=0,
            concat_axis=1,
            tiled=True,
        ),
        lax.all_to_all(
            value_grad.reshape(all_tokens, local_heads * HD),
            "seq",
            split_axis=0,
            concat_axis=1,
            tiled=True,
        ),
    )
    key_out = (
        key_home.reshape(token_rows, KVH, group_size, HD)
        .sum(axis=2)
        .reshape(token_rows, kv_width)
        .astype(jnp.bfloat16)
    )
    value_out = (
        value_home.reshape(token_rows, KVH, group_size, HD)
        .sum(axis=2)
        .reshape(token_rows, kv_width)
        .astype(jnp.bfloat16)
    )
    gate_grad = lax.psum(gate_term, ("seq", "dp"))
    return (
        cross_grad[None],
        gate_grad,
        block_grad[None, None],
        self_grad[None],
        key_out[None],
        value_out[None],
    )


def solution(mesh):
    in_specs = (
        P("dp", "seq", None),
        P("dp", "seq", None),
        P(),
        P("dp", "seq", None, None),
        P("dp", "seq"),
        P("dp", "seq", None),
        P("dp", "seq", None),
        P("dp", "seq", None),
        P("dp", "seq", None),
        P("dp", "seq"),
    )
    out_specs = (
        P("dp", "seq", None),
        P(),
        P("dp", "seq", None, None),
        P("dp", "seq", None),
        P("dp", "seq", None),
        P("dp", "seq", None),
    )
    return jax.shard_map(local, mesh=mesh, in_specs=in_specs, out_specs=out_specs, check_vma=False)
```

profile of v0, /device:TPU:6, one launch (start us, length us, event | category | flops | bytes accessed | tf_op | source)
XLA Modules:
  0.0 659.0 jit_solution(18215347309455087132)
XLA Ops:
  0.6 2.4 copy.90
  3.0 7.7 %all-to-all-start = ((bf16[128,32,128]{0,2,1:T(8,128)(2,1)}), bf16[128,32,128]{0,2,1:T(8,128)(2,1)S(1)}, u32[]{:S(2)}, u32[]{:S(2)}) async-start(bf16[128,32,128]{0,2,1:T(8,128)(2,1)} %bitcast.28), calls=%async_computation | async-start | bytes 2097152 | tf_op jit(solution)/shard_map/all_to_all | solution.py:193
  12.0 13.3 %all-to-all-done = bf16[128,32,128]{0,2,1:T(8,128)(2,1)S(1)} async-done(((bf16[128,32,128]{0,2,1:T(8,128)(2,1)}), bf16[128,32,128]{0,2,1:T(8,128)(2,1)S(1)}, u32[]{:S(2)}, u32[]{:S(2)}) %all-to-all-start) | async-done | bytes 1048608 | tf_op jit(solution)/shard_map/all_to_all | solution.py:193
  25.3 6.6 all-to-all-start.2
  32.0 14.6 %all-to-all-done.2 = bf16[128,32,128]{0,2,1:T(8,128)(2,1)S(1)} async-done(((bf16[128,32,128]{0,2,1:T(8,128)(2,1)}), bf16[128,32,128]{0,2,1:T(8,128)(2,1)S(1)}, u32[]{:S(2)}, u32[]{:S(2)}) %all-to-all-start.2) | async-done | bytes 1048608 | tf_op jit(solution)/shard_map/all_to_all | solution.py:196
  47.8 6.6 all-to-all-start.1
  55.3 13.7 %all-to-all-done.1 = bf16[128,32,128]{2,0,1:T(8,128)(2,1)S(1)} async-done(((bf16[128,32,128]{2,0,1:T(8,128)(2,1)}), bf16[128,32,128]{2,0,1:T(8,128)(2,1)S(1)}, u32[]{:S(2)}, u32[]{:S(2)}) %all-to-all-start.1) | async-done | bytes 1048608 | tf_op jit(solution)/shard_map/all_to_all | solution.py:194
  70.3 7.3 %all-to-all-start.3 = ((bf16[128,32,128]{2,0,1:T(8,128)(2,1)}), bf16[128,32,128]{2,0,1:T(8,128)(2,1)}, u32[]{:S(2)}, u32[]{:S(2)}) async-start(bf16[128,32,128]{2,0,1:T(8,128)(2,1)} %bitcast.38), calls=%async_computation.3 | async-start | bytes 2097152 | tf_op jit(solution)/shard_map/all_to_all | solution.py:195
  77.7 2.1 collective-permute-start
  80.4 2.3 copy.82
  82.7 2.3 copy.84
  85.1 51.8 %all-gather = s32[1,4096]{1,0:T(1,128)S(1)} all-gather(s32[1,128]{1,0:T(1,128)S(1)} %copy-done.13), channel_id=2, replica_groups=mesh['seq'=32,'dp'=8] {'seq'}, dimensions={1}, use_global_device_ids=true | all-gather | bytes 16896 | tf_op jit(solution)/shard_map/all_gather | solution.py:183
  142.5 235.3 %while.34 = (s32[]{:T(128)}, f32[4096,1,128]{2,0,1:T(8,128)}, f32[4096,1,128]{2,0,1:T(8,128)}, bf16[16,256,1,128]{3,1,0,2:T(8,128)(2,1)}, s32[16]{0:T(128)S(1)},...) while((s32[]{:T(128)}, f32[4096,1,128]{2,0,1:T(8,128)}, ...), condition=%wide.region_11.12_spmd.clone, body=%wide.region_7.11_spmd.clone.sunk | while | flops 306184448 | bytes 14714647 | solution.py:147
  192.3 1.9 dynamic_update_slice.54
  198.3 1.9 dynamic_update_slice.53
  207.1 1.9 dynamic_update_slice.54
  221.8 1.9 dynamic_update_slice.54
  251.2 1.9 dynamic_update_slice.54
  271.9 1.9 dynamic_update_slice.53
  280.6 1.9 dynamic_update_slice.54
  286.7 1.9 dynamic_update_slice.53
  301.4 1.9 dynamic_update_slice.53
  310.1 1.9 dynamic_update_slice.54
  316.1 1.9 dynamic_update_slice.53
  324.8 1.9 dynamic_update_slice.54
  345.6 1.9 dynamic_update_slice.53
  354.3 1.9 dynamic_update_slice.54
  377.8 3.0 copy.100
  380.8 6.4 all-to-all-start.4
  387.3 2.3 broadcast_select_fusion
  389.8 2.5 reshape.259
  392.3 2.5 reshape.261
  394.8 3.6 copy_bitcast_fusion
  398.3 3.7 all-to-all-done.4
  402.0 7.5 %all-to-all-start.5 = ((f32[32,128,128]{1,2,0:T(8,128)}), f32[32,128,128]{1,2,0:T(8,128)}, u32[]{:S(2)}, u32[]{:S(2)}) async-start(f32[32,128,128]{1,2,0:T(8,128)} %copy.100), calls=%async_computation.5 | async-start | bytes 4194304 | tf_op jit(solution)/shard_map/all_to_all | solution.py:216
  409.6 74.3 %while.33 = (s32[]{:T(128)}, bf16[4,128,8,128]{3,1,2,0:T(8,128)(2,1)S(1)}, f32[4,1601,128]{2,1,0:T(8,128)}, f32[4,1601,128]{2,1,0:T(8,128)}, f32[4,8]{1,0:T(4,12...) while((s32[]{:T(128)}, ...), condition=%wide.region_5.6_spmd, body=%wide.region_0.5_spmd.sunk | while | flops 2534558208 | bytes 70913416 | solution.py:68
  409.6 5.8 fusion.166
  415.4 3.6 fusion.167
  421.9 1.9 fusion.171
  423.9 2.2 fusion.170
  426.1 2.0 fusion.172
  428.1 5.8 fusion.166
  433.9 3.6 fusion.167
  440.5 1.9 fusion.171
  442.4 2.2 fusion.170
  444.6 2.1 fusion.172
  446.7 5.8 fusion.166
  452.5 3.6 fusion.167
  459.1 1.9 fusion.171
  461.0 2.2 fusion.170
  463.2 2.1 fusion.172
  465.3 5.8 fusion.166
  471.1 3.6 fusion.167
  477.7 1.9 fusion.171
  479.6 2.2 fusion.170
  481.8 2.0 fusion.172
  483.9 6.5 copy.88
  493.0 5.1 copy.89
  500.0 2.7 select_convert_fusion
  503.9 2.5 collective-permute-start.1
  508.3 8.2 %all-to-all-start.6 = ((f32[32,128,128]{1,2,0:T(8,128)}), f32[32,128,128]{1,2,0:T(8,128)S(1)}, u32[]{:S(2)}, u32[]{:S(2)}) async-start(f32[32,128,128]{1,2,0:T(8,128)} %copy.104), calls=%async_computation.6 | async-start | bytes 4194304 | tf_op jit(solution)/shard_map/all_to_all | solution.py:223
  522.0 48.4 %all-to-all-done.6 = f32[32,128,128]{1,2,0:T(8,128)S(1)} async-done(((f32[32,128,128]{1,2,0:T(8,128)}), f32[32,128,128]{1,2,0:T(8,128)S(1)}, u32[]{:S(2)}, u32[]{:S(2)}) %all-to-all-start.6) | async-done | bytes 2097184 | tf_op jit(solution)/shard_map/all_to_all | solution.py:223
  571.3 80.7 %psum.7 = f32[32]{0:T(128)} all-reduce(f32[32]{0:T(128)S(1)} %broadcast_select_fusion.1), channel_id=1, replica_groups=mesh['seq'=32,'dp'=8] {'seq','dp'}, use_global_device_ids=true, to_apply=%region_6.7 | all-reduce | flops 32 | bytes 256 | tf_op jit(solution)/shard_map/psum | solution.py:243
  654.1 4.9 fusion.101
  (474 shorter events, 235.6 us)
Async XLA Ops:
  0.6 10.1 %copy-start.11 = (bf16[1,128,4096]{2,1,0:T(8,128)(2,1)S(1)}, bf16[1,128,4096]{2,1,0:T(8,128)(2,1)}, u32[]{:S(2)}) copy-start(bf16[1,128,4096]{2,1,0:T(8,128)(2,1)} %param.22) | copy-start | bytes 3145732
  3.0 28.9 %copy-start.12 = (bf16[1,128,512]{2,1,0:T(8,128)(2,1)S(1)}, bf16[1,128,512]{2,1,0:T(8,128)(2,1)}, u32[]{:S(2)}) copy-start(bf16[1,128,512]{2,1,0:T(8,128)(2,1)} %param.20) | copy-start | bytes 393220
  3.0 22.3 %all-to-all-start = ((bf16[128,32,128]{0,2,1:T(8,128)(2,1)}), bf16[128,32,128]{0,2,1:T(8,128)(2,1)S(1)}, u32[]{:S(2)}, u32[]{:S(2)}) async-start(bf16[128,32,128]{0,2,1:T(8,128)(2,1)} %bitcast.28), calls=%async_computation | async-start | bytes 2097152 | tf_op jit(solution)/shard_map/all_to_all | solution.py:193
  25.3 21.3 %all-to-all-start.2 = ((bf16[128,32,128]{0,2,1:T(8,128)(2,1)}), bf16[128,32,128]{0,2,1:T(8,128)(2,1)S(1)}, u32[]{:S(2)}, u32[]{:S(2)}) async-start(bf16[128,32,128]{0,2,1:T(8,128)(2,1)} %bitcast.35), calls=%async_computation.2 | async-start | bytes 2097152 | tf_op jit(solution)/shard_map/all_to_all | solution.py:196
  47.8 21.3 %all-to-all-start.1 = ((bf16[128,32,128]{2,0,1:T(8,128)(2,1)}), bf16[128,32,128]{2,0,1:T(8,128)(2,1)S(1)}, u32[]{:S(2)}, u32[]{:S(2)}) async-start(bf16[128,32,128]{2,0,1:T(8,128)(2,1)} %bitcast.32), calls=%async_computation.1 | async-start | bytes 2097152 | tf_op jit(solution)/shard_map/all_to_all | solution.py:194
  70.3 14.7 %copy-start.14 = (f32[32]{0:T(128)S(1)}, f32[32]{0:T(128)}, u32[]{:S(2)}) copy-start(f32[32]{0:T(128)} %param.16) | copy-start | bytes 388
  70.3 14.8 %copy-start.13 = (s32[1,128]{1,0:T(1,128)S(1)}, s32[1,128]{1,0:T(1,128)}, u32[]{:S(2)}) copy-start(s32[1,128]{1,0:T(1,128)} %param.23) | copy-start | bytes 1540
  70.3 69.2 %all-to-all-start.3 = ((bf16[128,32,128]{2,0,1:T(8,128)(2,1)}), bf16[128,32,128]{2,0,1:T(8,128)(2,1)}, u32[]{:S(2)}, u32[]{:S(2)}) async-start(bf16[128,32,128]{2,0,1:T(8,128)(2,1)} %bitcast.38), calls=%async_computation.3 | async-start | bytes 2097152 | tf_op jit(solution)/shard_map/all_to_all | solution.py:195
  77.7 309.6 %collective-permute-start = (bf16[1601,1024]{1,0:T(8,128)(2,1)}, bf16[1601,1024]{1,0:T(8,128)(2,1)}, u32[]{:S(2)}, u32[]{:S(2)}) collective-permute-start(bf16[1601,1024]{1,0:T(8,128)(2,1)} %bitcast.273), channel_id=1, source_target_pairs={{0,8},{8,16},{16,24},{24,32},{32,40},{40,48},{48,56},{56,64},{64,7... | collective-permute-start | bytes 9836552 | tf_op jit(solution)/shard_map/ppermute | solution.py:20
  377.8 9.5 %copy-start.5 = (bf16[1,1,1601,1024]{3,2,1,0:T(8,128)(2,1)S(1)}, bf16[1,1,1601,1024]{3,2,1,0:T(8,128)(2,1)}, u32[]{:S(2)}) copy-start(bf16[1,1,1601,1024]{3,2,1,0:T(8,128)(2,1)} %param.17) | copy-start | bytes 9836548
  380.8 21.2 %all-to-all-start.4 = ((bf16[32,128,128]{2,1,0:T(8,128)(2,1)}), bf16[32,128,128]{2,1,0:T(8,128)(2,1)}, u32[]{:S(2)}, u32[]{:S(2)}) async-start(bf16[32,128,128]{2,1,0:T(8,128)(2,1)} %bitcast.276), calls=%async_computation.4 | async-start | bytes 2097152 | tf_op jit(solution)/shard_map/all_to_all | solution.py:208
  392.3 2.5 copy-start.2
  398.3 11.2 %copy-start.3 = (bf16[1,128,4096]{1,2,0:T(8,128)(2,1)S(1)}, bf16[1,128,4096]{1,2,0:T(8,128)(2,1)}, u32[]{:S(2)}) copy-start(bf16[1,128,4096]{1,2,0:T(8,128)(2,1)} %copy.82) | copy-start | bytes 3145732
  398.3 11.2 %copy-start.4 = (bf16[1,128,4096]{1,2,0:T(8,128)(2,1)S(1)}, bf16[1,128,4096]{1,2,0:T(8,128)(2,1)}, u32[]{:S(2)}) copy-start(bf16[1,128,4096]{1,2,0:T(8,128)(2,1)} %copy.84) | copy-start | bytes 3145732
  398.3 11.2 %copy-start.8 = (bf16[4,128,8,128]{3,1,2,0:T(8,128)(2,1)S(1)}, bf16[4,128,8,128]{3,1,2,0:T(8,128)(2,1)}, u32[]{:S(2)}) copy-start(bf16[4,128,8,128]{3,1,2,0:T(8,128)(2,1)} %custom-call.1) | copy-start | bytes 3145732
  402.0 106.2 %all-to-all-start.5 = ((f32[32,128,128]{1,2,0:T(8,128)}), f32[32,128,128]{1,2,0:T(8,128)}, u32[]{:S(2)}, u32[]{:S(2)}) async-start(f32[32,128,128]{1,2,0:T(8,128)} %copy.100), calls=%async_computation.5 | async-start | bytes 4194304 | tf_op jit(solution)/shard_map/all_to_all | solution.py:216
  415.4 4.6 slice-start
  415.4 3.6 copy-start.7
  415.4 5.3 slice-start.1
  433.9 4.6 slice-start
  433.9 3.6 copy-start.7
  433.9 5.3 slice-start.1
  452.5 4.6 slice-start
  452.5 3.6 copy-start.7
  452.5 5.3 slice-start.1
  471.1 4.6 slice-start
  471.1 3.6 copy-start.7
  471.1 5.3 slice-start.1
  483.9 7.2 %copy-start.9 = (bf16[4,128,8,128]{3,1,2,0:T(8,128)(2,1)}, bf16[4,128,8,128]{3,1,2,0:T(8,128)(2,1)S(1)}, u32[]{:S(2)}) copy-start(bf16[4,128,8,128]{3,1,2,0:T(8,128)(2,1)S(1)} %get-tuple-element.212) | copy-start | bytes 3145732
  491.0 1.9 copy-start.6
  500.0 3.9 copy-start
  500.0 6.5 copy-start.1
  503.9 150.2 %collective-permute-start.1 = (bf16[1601,1024]{1,0:T(8,128)(2,1)}, bf16[1601,1024]{1,0:T(8,128)(2,1)}, u32[]{:S(2)}, u32[]{:S(2)}) collective-permute-start(bf16[1601,1024]{1,0:T(8,128)(2,1)} %select_convert_fusion), channel_id=1, source_target_pairs={{8,0},{16,8},{24,16},{32,24},{40,32},{48,40},{56,48},{64,56},{72,6... | collective-permute-start | bytes 9836552 | tf_op jit(solution)/shard_map/ppermute | solution.py:20
  508.3 62.1 %all-to-all-start.6 = ((f32[32,128,128]{1,2,0:T(8,128)}), f32[32,128,128]{1,2,0:T(8,128)S(1)}, u32[]{:S(2)}, u32[]{:S(2)}) async-start(f32[32,128,128]{1,2,0:T(8,128)} %copy.104), calls=%async_computation.6 | async-start | bytes 4194304 | tf_op jit(solution)/shard_map/all_to_all | solution.py:223
  518.1 52.5 %copy-start.15 = (f32[32]{0:T(128)S(1)}, f32[32]{0:T(128)}, u32[]{:S(2)}) copy-start(f32[32]{0:T(128)} %param.16) | copy-start | bytes 388
  519.4 132.7 %copy-start.10 = (bf16[4,128,8,128]{3,1,2,0:T(8,128)(2,1)S(1)}, bf16[4,128,8,128]{3,1,2,0:T(8,128)(2,1)}, u32[]{:S(2)}) copy-start(bf16[4,128,8,128]{3,1,2,0:T(8,128)(2,1)} %copy-done.9) | copy-start | bytes 3145732
where the time goes:
time: 667 us; the launch traced here: 659 us
  local copies, waits for them, and re-layouts  187 us (28%)
  matrix products  146 us (22%)
  blocking collectives  133 us (20%)
  waiting for transfers between devices  93.7 us (14%)
  starting transfers between devices  54.8 us (8%)
  other arithmetic  30.8 us (5%)
  loops' own time  12.6 us (2%)
    psum x1, blocking collectives, local(): gate_grad = lax.psum(gate_term, ('seq', 'dp'))  80.7 us
    all_gather x1, blocking collectives, local(): docs = lax.all_gather(doc_ids[0], 'seq', axis=0, tiled=True)  51.8 us
    all_to_all x1, waiting for transfers between devices, local(): lax.all_to_all(value_grad.reshape(all_tokens, local_heads * HD), 'seq', s...  48.4 us
    dynamic_update_slice x32, local copies, waits for them, and re-layouts, step(): lax.dynamic_update_slice_in_dim(value_total, lax.dynamic_slice_in_dim(val...  32.1 us
    dynamic_update_slice x32, local copies, waits for them, and re-layouts, step(): lax.dynamic_update_slice_in_dim(key_total, lax.dynamic_slice_in_dim(key_t...  32 us
    sub x4, matrix products, one_head(): weights = jnp.exp(scores - row_max)  23.2 us
    dot_general x16, matrix products, step(): jnp.einsum('hqk,khd->qhd', weights_low, value_window, preferred_element_t...  22.1 us
    dynamic_slice x32, local copies, waits for them, and re-layouts, step(): lax.dynamic_slice_in_dim(value_total, key_start, window, 0) + value_grad  21.5 us
  transfers between devices with their start and end apart: 9, of which 5 were waited for; matrix products, arithmetic and copies ran while one was open for 53% of the time, Pallas kernels for 0%

commit v1 on v0

v1 whole, which is shorter than its diff:
```python
import math

import jax
import jax.numpy as jnp
from jax import lax
from jax.experimental import pallas as pl
from jax.experimental.pallas import tpu as pltpu
from jax.sharding import PartitionSpec as P

HEADS = 32
KVH = 4
HD = 128
GROUP = HEADS // KVH
VROWS = 1601
WHOLE = VROWS - 1
NK = 1616
TOK = 128
SPAN = 5
WIN = SPAN * TOK
NQ = GROUP * TOK
KVW = KVH * HD
FACTOR = HD**-0.5
EXP2 = FACTOR * math.log2(math.e)
NEG = -1e30
SUB = 16

F32 = jnp.float32
BF = jnp.bfloat16
NT = (((1,), (1,)), ((), ()))
NN = (((1,), (0,)), ((), ()))
MESH = pl.DeviceIdType.MESH


def dot(a, b, dims):
    return lax.dot_general(a, b, dims, preferred_element_type=F32)


def fold(x, op):
    total = x[0:8]
    for i in range(8, x.shape[0], 8):
        total = op(total, x[i : i + 8])
    return total


def key_phase(nk, k, q_s, c_s, tq_s, do_s, e_scr, eb, adjust, scale_row):
    scores = dot(k[...], q_s[...], NT)
    m8 = jnp.full((8, NQ), NEG, F32)
    for i in range(0, nk, SUB):
        x = adjust(i, scores[i : i + SUB])
        e_scr[pl.ds(i, SUB), :] = x
        m8 = jnp.maximum(m8, fold(x, jnp.maximum))
    m = jnp.max(m8, axis=0, keepdims=True) * EXP2
    l8 = jnp.zeros((8, NQ), F32)
    for i in range(0, nk, SUB):
        e = jnp.exp2(e_scr[pl.ds(i, SUB), :] * EXP2 - m)
        l8 = l8 + fold(e, jnp.add)
        e_scr[pl.ds(i, SUB), :] = e
        eb[pl.ds(i, SUB), :] = e.astype(BF)
    r = 1.0 / jnp.sum(l8, axis=0, keepdims=True)
    for h in range(GROUP):
        rows = slice(h * TOK, h * TOK + TOK)
        wide = jnp.broadcast_to(scale_row(h, r[:, rows]), (TOK, HD)).T
        tq_s[rows, :] = (q_s[rows, :].astype(F32) * wide).astype(BF)
        do_s[rows, :] = (c_s[rows, :].astype(F32) * wide).astype(BF)
    return r


def value_phase(nk, v, c_s, e_scr, d_scr, ds, r):
    raw = dot(v[...], c_s[...], NT)
    e8 = jnp.zeros((8, NQ), F32)
    for i in range(0, nk, SUB):
        d = raw[i : i + SUB]
        e8 = e8 + fold(e_scr[pl.ds(i, SUB), :] * d, jnp.add)
        d_scr[pl.ds(i, SUB), :] = d
    inner = jnp.sum(e8, axis=0, keepdims=True) * r
    for i in range(0, nk, SUB):
        ds[pl.ds(i, SUB), :] = (e_scr[pl.ds(i, SUB), :] * (d_scr[pl.ds(i, SUB), :] - inner)).astype(BF)
    return inner


def kernel(
    xq, xc, gate, vis, bmap, sq, sk, sv, sc, doc,
    xdq, esum, vgrad, sdq, kgrad, valgrad,
    recv, own, xq_v, xc_v, sq_v, sc_v, line, pair, dline, dpair,
    kp, vp, k_t, q_s, c_s, tq_s, do_s, e_scr, d_scr, eb, ds, bias,
    gown, gsend, garr, xdq_v, sdq_v, og, ag, bg, xs, xr, bs, br, as_, ar,
    ld_sem, own_sem, out_sem, v_ss, v_rs, h_ss, h_rs, d_ss, d_rs, g_ss, g_rs, s_ss, s_rs,
):
    count = lax.axis_size("seq")
    me = lax.axis_index("seq")
    par = lax.rem(me, 2)
    next1, prev1 = lax.rem(me + 1, count), lax.rem(me + count - 1, count)
    next2, prev2 = lax.rem(me + 2, count), lax.rem(me + count - 2, count)
    other = me + 1 - 2 * par
    bm = bmap[0, 0]

    def remote(src, dst, send, arrive, device):
        return pltpu.make_async_remote_copy(
            src_ref=src, dst_ref=dst, send_sem=send, recv_sem=arrive,
            device_id={"seq": device}, device_id_type=MESH,
        )

    barrier = pltpu.get_barrier_semaphore()
    for device in (next1, prev1, next2, prev2):
        pl.semaphore_signal(barrier, inc=1, device_id={"seq": device}, device_id_type=MESH)

    loads = [
        pltpu.make_async_copy(sk.at[0], line.at[0, 0], ld_sem.at[0]),
        pltpu.make_async_copy(sv.at[0], line.at[0, 1], ld_sem.at[1]),
        pltpu.make_async_copy(sq.at[0], sq_v, ld_sem.at[2]),
        pltpu.make_async_copy(sc.at[0], sc_v, ld_sem.at[3]),
        pltpu.make_async_copy(xq.at[0], xq_v, ld_sem.at[4]),
        pltpu.make_async_copy(xc.at[0], xc_v, ld_sem.at[5]),
    ]
    for copy in loads:
        copy.start()
    parts = []
    for h in range(KVH):
        for half in range(2):
            column = pl.ds(half * KVW + h * HD, HD)
            parts.append((2 * h + half, vis.at[0, 0, :, column]))
    for i, src in parts:
        pltpu.make_async_copy(src, own.at[i], own_sem.at[i]).start()
    dline[0] = jnp.broadcast_to(doc[...], (8, TOK))
    pl.semaphore_wait(barrier, 4)

    first = [
        remote(sk.at[0], line.at[1, 0], h_ss.at[0], h_rs.at[0], next2),
        remote(sv.at[0], line.at[1, 1], h_ss.at[1], h_rs.at[1], next2),
        remote(dline.at[0], dline.at[1], d_ss.at[0], d_rs.at[0], next2),
    ]
    for copy in (first[2], first[0], first[1]):
        copy.start()
    relay = [
        remote(line.at[1, 0], line.at[2, 0], h_ss.at[2], h_rs.at[2], next2),
        remote(line.at[1, 1], line.at[2, 1], h_ss.at[3], h_rs.at[3], next2),
        remote(dline.at[1], dline.at[2], d_ss.at[1], d_rs.at[1], next2),
    ]
    for i in (2, 0, 1):
        first[i].wait_recv()
        relay[i].start()
    for i, src in parts:
        remote(src, recv.at[i], v_ss.at[i], v_rs.at[i], next1).start()
    loads[0].wait()
    loads[1].wait()
    share = [
        remote(line.at[par], pair.at[0], h_ss.at[4], h_rs.at[4], other),
        remote(dline.at[par], dpair.at[0], d_ss.at[2], d_rs.at[2], other),
        remote(line.at[par + 1], pair.at[1], h_ss.at[5], h_rs.at[5], other),
        remote(dline.at[par + 1], dpair.at[1], d_ss.at[3], d_rs.at[3], other),
    ]
    share[0].start()
    share[1].start()
    for i in (2, 0, 1):
        relay[i].wait_recv()
    share[2].start()
    share[3].start()
    for copy in share:
        copy.wait_recv()
    for copy in loads[2:]:
        copy.wait()

    mine = dline[0, 0:1, :].astype(F32)
    lanes = lax.broadcasted_iota(jnp.int32, (TOK, TOK), 1)
    sublanes = lax.broadcasted_iota(jnp.int32, (TOK, TOK), 0)
    docs = (dline[0, 0:1, :], dpair[0, 0:1, :], dline[1, 0:1, :], dpair[1, 0:1, :], dline[2, 0:1, :])
    for back, row in enumerate(docs):
        theirs = jnp.broadcast_to(row.astype(F32), (TOK, TOK)).T
        limit = jnp.where(me >= back, TOK if back else 0, -2 * TOK)
        allowed = (theirs == mine) & (sublanes <= lanes + limit)
        bias[pl.ds(back * TOK, TOK), :] = jnp.where(allowed, 0.0, NEG)

    def gather_heads(group, queries, cots):
        for h in range(GROUP):
            rows = slice(h * TOK, h * TOK + TOK)
            column = pl.ds(pl.multiple_of(group * NQ + h * HD, HD), HD)
            q_s[rows, :] = queries[:, column]
            c_s[rows, :] = cots[:, column]

    def transposed(src, nk):
        for i in range(0, nk, TOK):
            n = min(TOK, nk - i)
            tile = src[pl.ds(i, n), :]
            if n < TOK:
                tile = jnp.concatenate([tile, jnp.zeros((TOK - n, HD), BF)], axis=0)
            k_t[:, i : i + TOK] = tile.T

    blocks = ((line, 0), (pair, 0), (line, 1), (pair, 1), (line, 2))

    def self_group(g, carry):
        column = pl.ds(pl.multiple_of(g * HD, HD), HD)
        gather_heads(g, sq_v, sc_v)
        for b, (ref, slot) in enumerate(blocks):
            rows = pl.ds(b * TOK, TOK)
            kp[rows, :] = ref[slot, 0, :, column]
            vp[rows, :] = ref[slot, 1, :, column]
        k = kp.at[pl.ds(0, WIN)]
        transposed(k, WIN)

        def adjust(i, x):
            return x + jnp.concatenate([bias[pl.ds(i, SUB), :]] * GROUP, axis=1)

        eb_w, ds_w = eb.at[pl.ds(0, WIN)], ds.at[pl.ds(0, WIN)]
        r = key_phase(WIN, k, q_s, c_s, tq_s, do_s, e_scr, eb_w, adjust, lambda h, x: x)
        value_grad = dot(eb_w[...], do_s[...], NN)
        value_phase(WIN, vp.at[pl.ds(0, WIN)], c_s, e_scr, d_scr, ds_w, r)
        key_grad = dot(ds_w[...], tq_s[...], NN) * FACTOR
        dq_t = dot(k_t[:, 0:WIN], ds_w[...], NN)
        for h in range(GROUP):
            lane = slice(h * TOK, h * TOK + TOK)
            out = pl.ds(pl.multiple_of(g * NQ + h * HD, HD), HD)
            sdq_v[:, out] = (dq_t[:, lane] * (r[:, lane] * FACTOR)).T.astype(BF)
        for half, grad in enumerate((key_grad, value_grad)):
            og[half, :, column] = grad[0:TOK]
            xs[0, half, :, column] = grad[TOK : 2 * TOK].astype(BF)
            ag[half, :, column] = grad[2 * TOK : 3 * TOK]
            xs[1, half, :, column] = grad[3 * TOK : 4 * TOK].astype(BF)
            bg[half, :, column] = grad[4 * TOK : 5 * TOK]
        return carry

    lax.fori_loop(0, KVH, self_group, 0)
    swap = remote(xs, xr, s_ss.at[0], s_rs.at[0], other)
    far = remote(bs, br, s_ss.at[1], s_rs.at[1], prev2)
    near = remote(as_, ar, s_ss.at[2], s_rs.at[2], prev2)
    swap.start()
    sdq_out = pltpu.make_async_copy(sdq_v, sdq.at[0], out_sem.at[0])
    sdq_out.start()

    def grad_copy(i):
        return remote(gsend.at[i], garr.at[i], g_ss.at[i], g_rs.at[i], prev1)

    def load_part(dst, i):
        pltpu.make_async_copy(vis.at[0, 0, :, pl.ds(0, HD)], own.at[i], own_sem.at[i]).wait()
        remote(vis.at[0, 0, :, pl.ds(0, HD)], recv.at[i], v_ss.at[i], v_rs.at[i], next1).wait_recv()
        for b in range(0, WHOLE, 320):
            rows = pl.ds(b, 320)
            dst[rows, :] = jnp.where(bm == 1, recv[i, rows, :], own[i, rows, :])
        last = jnp.where(bm == 1, recv[i, pl.ds(WHOLE, 1), :].astype(F32), own[i, pl.ds(WHOLE, 1), :].astype(F32))
        top = lax.broadcasted_iota(jnp.int32, (NK - WHOLE, HD), 0) < 1
        dst[pl.ds(WHOLE, NK - WHOLE), :] = jnp.where(top, jnp.broadcast_to(last, (NK - WHOLE, HD)), 0.0).astype(BF)

    def send_grad(i, grad):
        keep = jnp.where(bm == 0, 1.0, 0.0).astype(F32)
        give = jnp.where(bm == 1, 1.0, 0.0).astype(F32)
        for b, n in ((0, 400), (400, 400), (800, 400), (1200, 400), (WHOLE, 1)):
            part = grad[b : b + n]
            gown[i, pl.ds(b, n), :] = part * keep
            gsend[i, pl.ds(b, n), :] = (part * give).astype(BF)
        grad_copy(i).start()

    def finish_part(i):
        grad_copy(i).wait_recv()
        for b, n in ((0, 400), (400, 400), (800, 400), (1200, 400), (WHOLE, 1)):
            rows = pl.ds(b, n)
            own[i, rows, :] = (gown[i, rows, :] + garr[i, rows, :].astype(F32)).astype(BF)

    def cross_group(h, carry):
        gather_heads(h, xq_v, xc_v)
        load_part(kp, 2 * h)
        transposed(kp, NK)
        gates = [jnp.tanh(jnp.full((1, TOK), gate[h * GROUP + j], F32)) for j in range(GROUP)]
        live = jnp.where(bm == 2, 0.0, 1.0).astype(F32)

        def adjust(i, x):
            if i + SUB <= VROWS:
                return x
            return jnp.where(lax.broadcasted_iota(jnp.int32, x.shape, 0) < VROWS - i, x, NEG)

        r = key_phase(NK, kp, q_s, c_s, tq_s, do_s, e_scr, eb, adjust, lambda j, x: x * gates[j])
        send_grad(2 * h + 1, dot(eb[...], do_s[...], NN))
        load_part(vp, 2 * h + 1)
        inner = value_phase(NK, vp, c_s, e_scr, d_scr, ds, r)
        send_grad(2 * h, dot(ds[...], tq_s[...], NN) * FACTOR)
        dq_t = dot(k_t[:, 0:NK], ds[...], NN)
        for j in range(GROUP):
            lane = slice(j * TOK, j * TOK + TOK)
            out = pl.ds(pl.multiple_of(h * NQ + j * HD, HD), HD)
            xdq_v[:, out] = (dq_t[:, lane] * (r[:, lane] * gates[j] * (live * FACTOR))).T.astype(BF)
            esum[pl.ds(h * GROUP + j, 1), :] = inner[:, lane] * ((1.0 - gates[j] * gates[j]) * live)

        @pl.when(h == 0)
        def _():
            swap.wait()
            even = jnp.where(par == 0, 1.0, 0.0).astype(F32)
            odd = 1.0 - even
            for half in range(2):
                x0, x1 = xr[0, half].astype(F32), xr[1, half].astype(F32)
                og[half] = og[half] + even * x0
                ag[half] = ag[half] + (odd * x0 + even * x1)
                bs[half] = (bg[half] + odd * x1).astype(BF)
            far.start()

        @pl.when(h == 1)
        def _():
            far.wait()
            for half in range(2):
                as_[half] = (ag[half] + br[half].astype(F32)).astype(BF)
            near.start()

        return carry

    lax.fori_loop(0, KVH, cross_group, 0)
    xdq_out = pltpu.make_async_copy(xdq_v, xdq.at[0], out_sem.at[1])
    xdq_out.start()
    near.wait()
    for half, out in enumerate((kgrad, valgrad)):
        out[0] = (og[half] + ar[half].astype(F32)).astype(BF)

    def part_out(i, column):
        return pltpu.make_async_copy(own.at[i], vgrad.at[0, 0, :, pl.ds(column, HD)], own_sem.at[i])

    for h in range(KVH):
        for half in (1, 0):
            i = 2 * h + half
            finish_part(i)
            part_out(i, half * KVW + h * HD).start()
    for h in range(KVH):
        for half in (1, 0):
            part_out(2 * h + half, half * KVW + h * HD).wait()
            grad_copy(2 * h + half).wait_send()
    for i, src in parts:
        remote(src, recv.at[i], v_ss.at[i], v_rs.at[i], next1).wait_send()
    for copy in first + relay + share:
        copy.wait_send()
    sdq_out.wait()
    xdq_out.wait()


def fused(*operands):
    anywhere = pl.BlockSpec(memory_space=pl.ANY)
    vmem = pl.BlockSpec(memory_space=pltpu.VMEM)
    smem = pl.BlockSpec(memory_space=pltpu.SMEM)
    wide = (1, TOK, HEADS * HD)
    shape = jax.ShapeDtypeStruct
    dma = pltpu.SemaphoreType.DMA
    vm = pltpu.VMEM
    return pl.pallas_call(
        kernel,
        in_specs=[anywhere, anywhere, smem, anywhere, smem, anywhere, anywhere, anywhere, anywhere, vmem],
        out_specs=[anywhere, vmem, anywhere, anywhere, vmem, vmem],
        out_shape=[
            shape(wide, BF),
            shape((HEADS, TOK), F32),
            shape((1, 1, VROWS, 2 * KVW), BF),
            shape(wide, BF),
            shape((1, TOK, KVW), BF),
            shape((1, TOK, KVW), BF),
        ],
        scratch_shapes=[
            vm((2 * KVH, VROWS, HD), BF),
            vm((2 * KVH, VROWS, HD), BF),
            *[vm((TOK, HEADS * HD), BF)] * 4,
            vm((3, 2, TOK, KVW), BF),
            vm((2, 2, TOK, KVW), BF),
            vm((3, 8, TOK), jnp.int32),
            vm((2, 8, TOK), jnp.int32),
            vm((NK, HD), BF),
            vm((NK, HD), BF),
            vm((HD, 1664), BF),
            *[vm((NQ, HD), BF)] * 4,
            *[vm((NK, NQ), F32)] * 2,
            *[vm((NK, NQ), BF)] * 2,
            vm((WIN, TOK), F32),
            vm((2 * KVH, VROWS, HD), F32),
            *[vm((2 * KVH, VROWS, HD), BF)] * 2,
            *[vm((TOK, HEADS * HD), BF)] * 2,
            *[vm((2, TOK, KVW), F32)] * 3,
            *[vm((2, 2, TOK, KVW), BF)] * 2,
            *[vm((2, TOK, KVW), BF)] * 4,
            dma((6,)),
            dma((2 * KVH,)),
            dma((2,)),
            *[dma((2 * KVH,))] * 2,
            *[dma((6,))] * 2,
            *[dma((4,))] * 2,
            *[dma((2 * KVH,))] * 2,
            *[dma((3,))] * 2,
        ],
        compiler_params=pltpu.CompilerParams(
            collective_id=0, has_side_effects=True, vmem_limit_bytes=60 * 2**20
        ),
        cost_estimate=pl.CostEstimate(flops=2 * 5 * NQ * KVH * HD * (NK + WIN), bytes_accessed=14 * 2**20, transcendentals=0),
    )(*operands)


def local(*operands):
    xdq, esum, vgrad, sdq, kgrad, valgrad = fused(*operands)
    gate_grad = lax.psum(jnp.sum(esum, axis=1), ("seq", "dp"))
    return xdq, gate_grad, vgrad, sdq, kgrad, valgrad


def solution(mesh):
    rows = P("dp", "seq", None)
    block = P("dp", "seq", None, None)
    return jax.shard_map(
        local,
        mesh=mesh,
        in_specs=(rows, rows, P(), block, P("dp", "seq"), rows, rows, rows, rows, P("dp", "seq")),
        out_specs=(rows, P(), block, rows, rows, rows),
        check_vma=False,
    )
```

time: 667 us -> 178 us (0.27)
  local copies, waits for them, and re-layouts: 187 us -> 8.65 us
  matrix products: 146 us -> 0 us
  waiting for transfers between devices: 93.7 us -> 0 us
  Pallas kernels: 0 us -> 80.9 us
  starting transfers between devices: 54.8 us -> 0 us
  blocking collectives: 133 us -> 83.1 us
  other arithmetic: 30.8 us -> 0.83 us
  loops' own time: 12.6 us -> 0 us
    dot_general x116 -> x0, matrix products: 123 us -> none  [the longest x16 22.1 us: step(): jnp.einsum('hqk,khd->qhd', weights_low, value_window, preferred_element_t...]
    all_to_all x7 -> x0, waiting for transfers between devices: 93.7 us -> none  [the longest x1 48.4 us: local(): lax.all_to_all(value_grad.reshape(all_tokens, local_heads * HD), 'seq', s...]
    pallas_call x0 -> x1, Pallas kernels: none -> 80.9 us  [fused(): pl.pallas_call(kernel, in_specs=[anywhere, anywhere, smem, anywhere, smem...]
    dynamic_update_slice x100 -> x0, local copies, waits for them, and re-layouts: 76.2 us -> none  [the longest x32 32.1 us: step(): lax.dynamic_update_slice_in_dim(value_total, lax.dynamic_slice_in_dim(val...]
    dynamic_slice x128 -> x0, local copies, waits for them, and re-layouts: 52.4 us -> none  [the longest x32 21.5 us: step(): lax.dynamic_slice_in_dim(value_total, key_start, window, 0) + value_grad]
    all_gather x1 -> x0, blocking collectives: 51.8 us -> none  [local(): docs = lax.all_gather(doc_ids[0], 'seq', axis=0, tiled=True)]
    all_to_all x7 -> x0, starting transfers between devices: 50.3 us -> none  [the longest x1 8.17 us: local(): lax.all_to_all(value_grad.reshape(all_tokens, local_heads * HD), 'seq', s...]
    sub x4 -> x0, matrix products: 23.2 us -> none  [one_head(): weights = jnp.exp(scores - row_max)]
  transfers between devices with their start and end apart: 9 -> 0, of which waited for: 5 -> 0; matrix products, arithmetic and copies ran while one was open for 53% -> 0% of each run, Pallas kernels for 0% -> 0%
where the time goes in v1:
time: 178 us; the launch traced here: 175 us
  blocking collectives  83.1 us (47%)
  Pallas kernels  80.9 us (45%)
  local copies, waits for them, and re-layouts  8.65 us (5%)
    psum x1, blocking collectives, local(): gate_grad = lax.psum(jnp.sum(esum, axis=1), ('seq', 'dp'))  83.1 us
    pallas_call x1, Pallas kernels, fused(): pl.pallas_call(kernel, in_specs=[anywhere, anywhere, smem, anywhere, smem...  80.9 us
    unnamed x11, local copies, waits for them, and re-layouts  8.65 us

profile of v1, /device:TPU:6, one launch (start us, length us, event | category | flops | bytes accessed | tf_op | source)
XLA Modules:
  0.0 174.8 jit_solution(1907242465684266048)
XLA Ops:
  1.3 80.9 %shard_map.145 = (bf16[1,128,4096]{2,1,0:T(8,128)(2,1)}, f32[32,128]{1,0:T(8,128)}, bf16[1,1,1601,1024]{3,2,1,0:T(8,128)(2,1)}, bf16[1,128,4096]{2,1,0:T(8,128)(...) custom-call(bf16[1,128,4096]{2,1,0:T(8,128)(2,1)} %xq.1, bf16[1,128,4096]{2,1,0:T(8,128)(2,1)} %xc.1, ...), custom_call_target="tpu_custom_call" | custom-call | flops 11827937280 | bytes 14680064 | tf_op jit(solution)/shard_map/pallas_call | solution.py:337
  82.2 0.8 reduce_sum.9
  83.1 83.1 %psum.7 = f32[32]{0:T(128)} all-reduce(f32[32]{0:T(128)S(1)} %reduce_sum.9), channel_id=1, replica_groups=mesh['seq'=32,'dp'=8] {'seq','dp'}, use_global_device_ids=true, to_apply=%region_1.0 | all-reduce | flops 32 | bytes 256 | tf_op jit(solution)/shard_map/psum | solution.py:388
  166.2 2.3 %copy.22 = bf16[1,128,4096]{2,1,0:T(8,128)(2,1)} copy(bf16[1,128,4096]{2,1,0:T(8,128)(2,1)} %get-tuple-element.24) | data formatting | bytes 2097152
  168.5 0.0 copy-start
  168.5 0.0 copy-start.2
  168.5 0.0 copy-start.1
  168.5 4.1 %copy.23 = bf16[1,1,1601,1024]{3,2,1,0:T(8,128)(2,1)} copy(bf16[1,1,1601,1024]{3,2,1,0:T(8,128)(2,1)} %get-tuple-element.26) | data formatting | bytes 6557696
  172.5 0.0 copy-done
  172.5 1.0 copy.24
  173.5 0.0 copy-done.2
  173.5 0.7 copy.25
  174.2 0.0 copy-done.1
  174.2 0.7 copy.26
Async XLA Ops:
  168.5 4.1 %copy-start = (bf16[1,128,4096]{2,1,0:T(8,128)(2,1)S(1)}, bf16[1,128,4096]{2,1,0:T(8,128)(2,1)}, u32[]{:S(2)}) copy-start(bf16[1,128,4096]{2,1,0:T(8,128)(2,1)} %get-tuple-element.27) | copy-start | bytes 3145732
  168.5 5.0 %copy-start.2 = (bf16[1,128,512]{2,1,0:T(8,128)(2,1)S(1)}, bf16[1,128,512]{2,1,0:T(8,128)(2,1)}, u32[]{:S(2)}) copy-start(bf16[1,128,512]{2,1,0:T(8,128)(2,1)} %get-tuple-element.28) | copy-start | bytes 393220
  168.5 5.7 %copy-start.1 = (bf16[1,128,512]{2,1,0:T(8,128)(2,1)S(1)}, bf16[1,128,512]{2,1,0:T(8,128)(2,1)}, u32[]{:S(2)}) copy-start(bf16[1,128,512]{2,1,0:T(8,128)(2,1)} %get-tuple-element.29) | copy-start | bytes 393220

commit v2 on v1

--- a/solution.py
+++ b/solution.py
@@ -23,11 +23,13 @@
 EXP2 = FACTOR * math.log2(math.e)
 NEG = -1e30
 SUB = 16
+ROW = 8
 
 F32 = jnp.float32
 BF = jnp.bfloat16
 NT = (((1,), (1,)), ((), ()))
 NN = (((1,), (0,)), ((), ()))
+TN = (((0,), (0,)), ((), ()))
 MESH = pl.DeviceIdType.MESH
 
 
@@ -42,7 +44,15 @@
     return total
 
 
-def key_phase(nk, k, q_s, c_s, tq_s, do_s, e_scr, eb, adjust, scale_row):
+def scale_rows(sums, source, group, target):
+    for h in range(GROUP):
+        rows = slice(h * TOK, h * TOK + TOK)
+        column = pl.ds(pl.multiple_of(group * NQ + h * HD, HD), HD)
+        wide = jnp.broadcast_to(sums[:, rows], (TOK, HD)).T
+        target[rows, :] = (source[:, column].astype(F32) * wide).astype(BF)
+
+
+def key_phase(nk, k, q_s, e_scr, eb, adjust):
     scores = dot(k[...], q_s[...], NT)
     m8 = jnp.full((8, NQ), NEG, F32)
     for i in range(0, nk, SUB):
@@ -56,13 +66,7 @@
         l8 = l8 + fold(e, jnp.add)
         e_scr[pl.ds(i, SUB), :] = e
         eb[pl.ds(i, SUB), :] = e.astype(BF)
-    r = 1.0 / jnp.sum(l8, axis=0, keepdims=True)
-    for h in range(GROUP):
-        rows = slice(h * TOK, h * TOK + TOK)
-        wide = jnp.broadcast_to(scale_row(h, r[:, rows]), (TOK, HD)).T
-        tq_s[rows, :] = (q_s[rows, :].astype(F32) * wide).astype(BF)
-        do_s[rows, :] = (c_s[rows, :].astype(F32) * wide).astype(BF)
-    return r
+    return 1.0 / jnp.sum(l8, axis=0, keepdims=True)
 
 
 def value_phase(nk, v, c_s, e_scr, d_scr, ds, r):
@@ -80,11 +84,11 @@
 
 def kernel(
     xq, xc, gate, vis, bmap, sq, sk, sv, sc, doc,
-    xdq, esum, vgrad, sdq, kgrad, valgrad,
+    xdq, gsum, vgrad, sdq, kgrad, valgrad,
     recv, own, xq_v, xc_v, sq_v, sc_v, line, pair, dline, dpair,
-    kp, vp, k_t, q_s, c_s, tq_s, do_s, e_scr, d_scr, eb, ds, bias,
+    kp, vp, k_t, q_s, c_s, tq_s, do_s, scores, eb, ds, bias, r_keep, esum, across, down, along,
     gown, gsend, garr, xdq_v, sdq_v, og, ag, bg, xs, xr, bs, br, as_, ar,
-    ld_sem, own_sem, out_sem, v_ss, v_rs, h_ss, h_rs, d_ss, d_rs, g_ss, g_rs, s_ss, s_rs,
+    ld_sem, own_sem, out_sem, v_ss, v_rs, h_ss, h_rs, d_ss, d_rs, g_ss, g_rs, s_ss, s_rs, a_ss, a_rs, b_ss, b_rs, c_ss, c_rs,
 ):
     count = lax.axis_size("seq")
     me = lax.axis_index("seq")
@@ -94,15 +98,26 @@
     other = me + 1 - 2 * par
     bm = bmap[0, 0]
 
-    def remote(src, dst, send, arrive, device):
+    def remote(src, dst, send, arrive, device, axis="seq"):
         return pltpu.make_async_remote_copy(
             src_ref=src, dst_ref=dst, send_sem=send, recv_sem=arrive,
-            device_id={"seq": device}, device_id_type=MESH,
+            device_id={axis: device}, device_id_type=MESH,
         )
 
+    depth = lax.axis_size("dp")
+    z = lax.axis_index("dp")
+    x, y = lax.rem(me, ROW), me // ROW
+    stages = (
+        (across, x, ROW, "seq", [y * ROW + lax.rem(x + i, ROW) for i in range(1, ROW)], a_ss, a_rs),
+        (down, y, count // ROW, "seq", [lax.rem(me + i * ROW, count) for i in range(1, count // ROW)], b_ss, b_rs),
+        (along, z, depth, "dp", [lax.rem(z + i, depth) for i in range(1, depth)], c_ss, c_rs),
+    )
+    partners = [("seq", device) for device in (next1, prev1, next2, prev2)]
+    for _, _, _, axis, devices, _, _ in stages:
+        partners += [(axis, device) for device in devices]
     barrier = pltpu.get_barrier_semaphore()
-    for device in (next1, prev1, next2, prev2):
-        pl.semaphore_signal(barrier, inc=1, device_id={"seq": device}, device_id_type=MESH)
+    for axis, device in partners:
+        pl.semaphore_signal(barrier, inc=1, device_id={axis: device}, device_id_type=MESH)
 
     loads = [
         pltpu.make_async_copy(sk.at[0], line.at[0, 0], ld_sem.at[0]),
@@ -122,41 +137,45 @@
     for i, src in parts:
         pltpu.make_async_copy(src, own.at[i], own_sem.at[i]).start()
     dline[0] = jnp.broadcast_to(doc[...], (8, TOK))
-    pl.semaphore_wait(barrier, 4)
+    esum[...] = jnp.zeros_like(esum)
+    pl.semaphore_wait(barrier, len(partners))
 
     first = [
         remote(sk.at[0], line.at[1, 0], h_ss.at[0], h_rs.at[0], next2),
         remote(sv.at[0], line.at[1, 1], h_ss.at[1], h_rs.at[1], next2),
         remote(dline.at[0], dline.at[1], d_ss.at[0], d_rs.at[0], next2),
     ]
-    for copy in (first[2], first[0], first[1]):
-        copy.start()
     relay = [
         remote(line.at[1, 0], line.at[2, 0], h_ss.at[2], h_rs.at[2], next2),
         remote(line.at[1, 1], line.at[2, 1], h_ss.at[3], h_rs.at[3], next2),
         remote(dline.at[1], dline.at[2], d_ss.at[1], d_rs.at[1], next2),
     ]
+    share0 = [
+        remote(line.at[par, 0], pair.at[0, 0], h_ss.at[4], h_rs.at[4], other),
+        remote(line.at[par, 1], pair.at[0, 1], h_ss.at[5], h_rs.at[5], other),
+        remote(dline.at[par], dpair.at[0], d_ss.at[2], d_rs.at[2], other),
+    ]
+    share1 = [
+        remote(line.at[par + 1, 0], pair.at[1, 0], h_ss.at[6], h_rs.at[6], other),
+        remote(line.at[par + 1, 1], pair.at[1, 1], h_ss.at[7], h_rs.at[7], other),
+        remote(dline.at[par + 1], dpair.at[1], d_ss.at[3], d_rs.at[3], other),
+    ]
+    for i in (2, 0, 1):
+        first[i].start()
+    loads[0].wait()
+    loads[1].wait()
     for i in (2, 0, 1):
         first[i].wait_recv()
         relay[i].start()
+        share0[i].start()
     for i, src in parts:
         remote(src, recv.at[i], v_ss.at[i], v_rs.at[i], next1).start()
-    loads[0].wait()
-    loads[1].wait()
-    share = [
-        remote(line.at[par], pair.at[0], h_ss.at[4], h_rs.at[4], other),
-        remote(dline.at[par], dpair.at[0], d_ss.at[2], d_rs.at[2], other),
-        remote(line.at[par + 1], pair.at[1], h_ss.at[5], h_rs.at[5], other),
-        remote(dline.at[par + 1], dpair.at[1], d_ss.at[3], d_rs.at[3], other),
-    ]
-    share[0].start()
-    share[1].start()
-    for i in (2, 0, 1):
+    for i in (2, 0):
         relay[i].wait_recv()
-    share[2].start()
-    share[3].start()
-    for copy in share:
-        copy.wait_recv()
+        share1[i].start()
+    for i in (2, 0):
+        share0[i].wait_recv()
+        share1[i].wait_recv()
     for copy in loads[2:]:
         copy.wait()
 
@@ -170,12 +189,10 @@
         allowed = (theirs == mine) & (sublanes <= lanes + limit)
         bias[pl.ds(back * TOK, TOK), :] = jnp.where(allowed, 0.0, NEG)
 
-    def gather_heads(group, queries, cots):
+    def gather_heads(group, source, target):
         for h in range(GROUP):
-            rows = slice(h * TOK, h * TOK + TOK)
             column = pl.ds(pl.multiple_of(group * NQ + h * HD, HD), HD)
-            q_s[rows, :] = queries[:, column]
-            c_s[rows, :] = cots[:, column]
+            target[h * TOK : h * TOK + TOK, :] = source[:, column]
 
     def transposed(src, nk):
         for i in range(0, nk, TOK):
@@ -187,38 +204,64 @@
 
     blocks = ((line, 0), (pair, 0), (line, 1), (pair, 1), (line, 2))
 
-    def self_group(g, carry):
+    eb_w, ds_w = eb.at[pl.ds(0, WIN)], ds.at[pl.ds(0, WIN)]
+    k_w, v_w = kp.at[pl.ds(0, WIN)], vp.at[pl.ds(0, WIN)]
+
+    def window(g, half, target):
         column = pl.ds(pl.multiple_of(g * HD, HD), HD)
-        gather_heads(g, sq_v, sc_v)
         for b, (ref, slot) in enumerate(blocks):
-            rows = pl.ds(b * TOK, TOK)
-            kp[rows, :] = ref[slot, 0, :, column]
-            vp[rows, :] = ref[slot, 1, :, column]
-        k = kp.at[pl.ds(0, WIN)]
-        transposed(k, WIN)
+            target[pl.ds(b * TOK, TOK), :] = ref[slot, half, :, column]
+
+    def spread(g, half, grad):
+        column = pl.ds(pl.multiple_of(g * HD, HD), HD)
+        og[half, :, column] = grad[0:TOK]
+        xs[0, half, :, column] = grad[TOK : 2 * TOK].astype(BF)
+        ag[half, :, column] = grad[2 * TOK : 3 * TOK]
+        xs[1, half, :, column] = grad[3 * TOK : 4 * TOK].astype(BF)
+        bg[half, :, column] = grad[4 * TOK : 5 * TOK]
+
+    def group_scores(g):
+        return scores.at[pl.ds(pl.multiple_of(g * WIN, WIN), WIN)]
+
+    def self_keys(g, carry):
+        gather_heads(g, sq_v, q_s)
+        window(g, 0, k_w)
 
         def adjust(i, x):
             return x + jnp.concatenate([bias[pl.ds(i, SUB), :]] * GROUP, axis=1)
 
-        eb_w, ds_w = eb.at[pl.ds(0, WIN)], ds.at[pl.ds(0, WIN)]
-        r = key_phase(WIN, k, q_s, c_s, tq_s, do_s, e_scr, eb_w, adjust, lambda h, x: x)
-        value_grad = dot(eb_w[...], do_s[...], NN)
-        value_phase(WIN, vp.at[pl.ds(0, WIN)], c_s, e_scr, d_scr, ds_w, r)
-        key_grad = dot(ds_w[...], tq_s[...], NN) * FACTOR
+        r = key_phase(WIN, k_w, q_s, group_scores(g), eb_w, adjust)
+        r_keep[g, 0:1, :] = r
+        scale_rows(r, sc_v, g, do_s)
+        spread(g, 1, dot(eb_w[...], do_s[...], NN))
+
+        @pl.when(g == 1)
+        def _():
+            relay[1].wait_recv()
+            share1[1].start()
+
+        return carry
+
+    def self_values(g, carry):
+        gather_heads(g, sc_v, c_s)
+        window(g, 0, k_w)
+        window(g, 1, v_w)
+        transposed(k_w, WIN)
+        r = r_keep[g, 0:1, :]
+        scale_rows(r, sq_v, g, tq_s)
+        value_phase(WIN, v_w, c_s, group_scores(g), scores.at[pl.ds(KVH * WIN, WIN)], ds_w, r)
+        spread(g, 0, dot(ds_w[...], tq_s[...], NN) * FACTOR)
         dq_t = dot(k_t[:, 0:WIN], ds_w[...], NN)
         for h in range(GROUP):
             lane = slice(h * TOK, h * TOK + TOK)
             out = pl.ds(pl.multiple_of(g * NQ + h * HD, HD), HD)
             sdq_v[:, out] = (dq_t[:, lane] * (r[:, lane] * FACTOR)).T.astype(BF)
-        for half, grad in enumerate((key_grad, value_grad)):
-            og[half, :, column] = grad[0:TOK]
-            xs[0, half, :, column] = grad[TOK : 2 * TOK].astype(BF)
-            ag[half, :, column] = grad[2 * TOK : 3 * TOK]
-            xs[1, half, :, column] = grad[3 * TOK : 4 * TOK].astype(BF)
-            bg[half, :, column] = grad[4 * TOK : 5 * TOK]
         return carry
 
-    lax.fori_loop(0, KVH, self_group, 0)
+    lax.fori_loop(0, KVH, self_keys, 0)
+    share0[1].wait_recv()
+    share1[1].wait_recv()
+    lax.fori_loop(0, KVH, self_values, 0)
     swap = remote(xs, xr, s_ss.at[0], s_rs.at[0], other)
     far = remote(bs, br, s_ss.at[1], s_rs.at[1], prev2)
     near = remote(as_, ar, s_ss.at[2], s_rs.at[2], prev2)
@@ -254,11 +297,47 @@
             rows = pl.ds(b, n)
             own[i, rows, :] = (gown[i, rows, :] + garr[i, rows, :].astype(F32)).astype(BF)
 
+    def stage_copy(number, i):
+        buffer, place, size, axis, devices, send, arrive = stages[number]
+        return remote(buffer.at[place], buffer.at[place], send.at[i], arrive.at[place], devices[i - 1], axis)
+
+    def stage_start(number, value):
+        buffer, place, size = stages[number][:3]
+        buffer[place] = jnp.broadcast_to(value, (8, TOK))
+        for i in range(1, size):
+            stage_copy(number, i).start()
+
+    def stage_end(number):
+        buffer, place, size, axis, devices, send, arrive = stages[number]
+        for i in range(1, size):
+            source = lax.rem(place + i, size)
+            remote(buffer.at[source], buffer.at[source], send.at[i], arrive.at[source], devices[i - 1], axis).wait_recv()
+        total = buffer[0, 0:1, :]
+        for i in range(1, size):
+            total = total + buffer[i, 0:1, :]
+        return total
+
+    def part_out(h, half):
+        column = pl.ds(pl.multiple_of(half * KVW + h * HD, HD), HD)
+        i = 2 * h + half
+        return pltpu.make_async_copy(own.at[i], vgrad.at[0, 0, :, column], own_sem.at[i])
+
+    def done_part(h, half):
+        finish_part(2 * h + half)
+        part_out(h, half).start()
+
+    def done_group(h):
+        done_part(h, 1)
+        done_part(h, 0)
+
+    e_scr, d_scr = scores.at[pl.ds(0, NK)], scores.at[pl.ds(NK, NK)]
+
     def cross_group(h, carry):
-        gather_heads(h, xq_v, xc_v)
+        gather_heads(h, xq_v, q_s)
+        gather_heads(h, xc_v, c_s)
         load_part(kp, 2 * h)
         transposed(kp, NK)
-        gates = [jnp.tanh(jnp.full((1, TOK), gate[h * GROUP + j], F32)) for j in range(GROUP)]
+        gates = jnp.concatenate([jnp.tanh(jnp.full((1, TOK), gate[h * GROUP + j], F32)) for j in range(GROUP)], axis=1)
         live = jnp.where(bm == 2, 0.0, 1.0).astype(F32)
 
         def adjust(i, x):
@@ -266,17 +345,27 @@
                 return x
             return jnp.where(lax.broadcasted_iota(jnp.int32, x.shape, 0) < VROWS - i, x, NEG)
 
-        r = key_phase(NK, kp, q_s, c_s, tq_s, do_s, e_scr, eb, adjust, lambda j, x: x * gates[j])
+        r = key_phase(NK, kp, q_s, e_scr, eb, adjust)
+        scale_rows(r * gates, xq_v, h, tq_s)
+        scale_rows(r * gates, xc_v, h, do_s)
         send_grad(2 * h + 1, dot(eb[...], do_s[...], NN))
         load_part(vp, 2 * h + 1)
         inner = value_phase(NK, vp, c_s, e_scr, d_scr, ds, r)
+        terms = inner * ((1.0 - gates * gates) * live)
+        for j in range(GROUP):
+            esum[pl.ds(h * GROUP + j, 1), :] = terms[:, j * TOK : j * TOK + TOK]
+
+        @pl.when(h == KVH - 1)
+        def _():
+            stage_start(0, jnp.sum(esum[...].T, axis=0, keepdims=True))
+
         send_grad(2 * h, dot(ds[...], tq_s[...], NN) * FACTOR)
         dq_t = dot(k_t[:, 0:NK], ds[...], NN)
+        factor = r * gates * (live * FACTOR)
         for j in range(GROUP):
             lane = slice(j * TOK, j * TOK + TOK)
             out = pl.ds(pl.multiple_of(h * NQ + j * HD, HD), HD)
-            xdq_v[:, out] = (dq_t[:, lane] * (r[:, lane] * gates[j] * (live * FACTOR))).T.astype(BF)
-            esum[pl.ds(h * GROUP + j, 1), :] = inner[:, lane] * ((1.0 - gates[j] * gates[j]) * live)
+            xdq_v[:, out] = (dq_t[:, lane] * factor[:, lane]).T.astype(BF)
 
         @pl.when(h == 0)
         def _():
@@ -290,6 +379,10 @@
                 bs[half] = (bg[half] + odd * x1).astype(BF)
             far.start()
 
+        @pl.when(h >= 2)
+        def _():
+            done_group(h - 2)
+
         @pl.when(h == 1)
         def _():
             far.wait()
@@ -302,25 +395,28 @@
     lax.fori_loop(0, KVH, cross_group, 0)
     xdq_out = pltpu.make_async_copy(xdq_v, xdq.at[0], out_sem.at[1])
     xdq_out.start()
+
     near.wait()
     for half, out in enumerate((kgrad, valgrad)):
         out[0] = (og[half] + ar[half].astype(F32)).astype(BF)
 
-    def part_out(i, column):
-        return pltpu.make_async_copy(own.at[i], vgrad.at[0, 0, :, pl.ds(column, HD)], own_sem.at[i])
-
+    stage_start(1, stage_end(0))
+    done_part(KVH - 2, 1)
+    done_part(KVH - 2, 0)
+    stage_start(2, stage_end(1))
+    done_part(KVH - 1, 1)
+    gsum[...] = stage_end(2)
+    done_part(KVH - 1, 0)
+    for number, stage in enumerate(stages):
+        for i in range(1, stage[2]):
+            stage_copy(number, i).wait_send()
     for h in range(KVH):
         for half in (1, 0):
-            i = 2 * h + half
-            finish_part(i)
-            part_out(i, half * KVW + h * HD).start()
-    for h in range(KVH):
-        for half in (1, 0):
-            part_out(2 * h + half, half * KVW + h * HD).wait()
+            part_out(h, half).wait()
             grad_copy(2 * h + half).wait_send()
     for i, src in parts:
         remote(src, recv.at[i], v_ss.at[i], v_rs.at[i], next1).wait_send()
-    for copy in first + relay + share:
+    for copy in first + relay + share0 + share1:
         copy.wait_send()
     sdq_out.wait()
     xdq_out.wait()
@@ -340,7 +436,7 @@
         out_specs=[anywhere, vmem, anywhere, anywhere, vmem, vmem],
         out_shape=[
             shape(wide, BF),
-            shape((HEADS, TOK), F32),
+            shape((1, TOK), F32),
             shape((1, 1, VROWS, 2 * KVW), BF),
             shape(wide, BF),
             shape((1, TOK, KVW), BF),
@@ -358,9 +454,12 @@
             vm((NK, HD), BF),
             vm((HD, 1664), BF),
             *[vm((NQ, HD), BF)] * 4,
-            *[vm((NK, NQ), F32)] * 2,
+            vm((2 * NK, NQ), F32),
             *[vm((NK, NQ), BF)] * 2,
             vm((WIN, TOK), F32),
+            vm((KVH, 8, NQ), F32),
+            vm((TOK, TOK), F32),
+            *[vm((8, 8, TOK), F32)] * 3,
             vm((2 * KVH, VROWS, HD), F32),
             *[vm((2 * KVH, VROWS, HD), BF)] * 2,
             *[vm((TOK, HEADS * HD), BF)] * 2,
@@ -371,10 +470,11 @@
             dma((2 * KVH,)),
             dma((2,)),
             *[dma((2 * KVH,))] * 2,
-            *[dma((6,))] * 2,
+            *[dma((8,))] * 2,
             *[dma((4,))] * 2,
             *[dma((2 * KVH,))] * 2,
             *[dma((3,))] * 2,
+            *[dma((8,))] * 6,
         ],
         compiler_params=pltpu.CompilerParams(
             collective_id=0, has_side_effects=True, vmem_limit_bytes=60 * 2**20
@@ -383,10 +483,33 @@
     )(*operands)
 
 
+def settle_kernel(*refs):
+    half = len(refs) // 2
+    for src, dst in zip(refs[:half], refs[half:]):
+        dst[...] = src[...]
+
+
+def settle(xdq, vgrad, sdq, kgrad, valgrad):
+    steps = 8
+    rows = TOK // steps
+    wide = pl.BlockSpec((1, rows, HEADS * HD), lambda i: (0, i, 0))
+    image = pl.BlockSpec((1, 1, 208, 2 * KVW), lambda i: (0, 0, i, 0))
+    narrow = pl.BlockSpec((1, rows, KVW), lambda i: (0, i, 0))
+    arrays = (xdq, vgrad, sdq, kgrad, valgrad)
+    specs = [wide, image, wide, narrow, narrow]
+    return pl.pallas_call(
+        settle_kernel,
+        grid=(steps,),
+        in_specs=specs,
+        out_specs=specs,
+        out_shape=[jax.ShapeDtypeStruct(x.shape, x.dtype) for x in arrays],
+    )(*arrays)
+
+
 def local(*operands):
-    xdq, esum, vgrad, sdq, kgrad, valgrad = fused(*operands)
-    gate_grad = lax.psum(jnp.sum(esum, axis=1), ("seq", "dp"))
-    return xdq, gate_grad, vgrad, sdq, kgrad, valgrad
+    xdq, gsum, vgrad, sdq, kgrad, valgrad = fused(*operands)
+    xdq, vgrad, sdq, kgrad, valgrad = settle(xdq, vgrad, sdq, kgrad, valgrad)
+    return xdq, gsum[0, :HEADS], vgrad, sdq, kgrad, valgrad
 
 
 def solution(mesh):

time: 178 us -> 109 us (0.61); the launches traced: 175 us -> 109 us
  blocking collectives: 83.1 us -> 0 us
  Pallas kernels: 80.9 us -> 107 us
  local copies, waits for them, and re-layouts: 8.65 us -> 0.52 us
    psum x1 -> x0, blocking collectives: 83.1 us -> none  [local(): gate_grad = lax.psum(jnp.sum(esum, axis=1), ('seq', 'dp'))]
    pallas_call x1, Pallas kernels: 80.9 us -> 99.5 us  [fused(): pl.pallas_call(kernel, in_specs=[anywhere, anywhere, smem, anywhere, smem...]
    unnamed x11 -> x2, local copies, waits for them, and re-layouts: 8.65 us -> 0.01 us
    pallas_call x0 -> x1, Pallas kernels: none -> 7.43 us  [settle(): pl.pallas_call(settle_kernel, grid=(steps,), in_specs=specs, out_specs=sp...]
where the time goes in v2:
time: 109 us
  Pallas kernels  107 us (98%)
  between operations  1.3 us (1%)
    pallas_call x1, Pallas kernels, fused(): pl.pallas_call(kernel, in_specs=[anywhere, anywhere, smem, anywhere, smem...  99.5 us
    pallas_call x1, Pallas kernels, settle(): pl.pallas_call(settle_kernel, grid=(steps,), in_specs=specs, out_specs=sp...  7.43 us

profile of v2, /device:TPU:6, one launch (start us, length us, event | category | flops | bytes accessed | tf_op | source)
XLA Modules:
  0.0 108.8 jit_solution(17227524206721915415)
XLA Ops:
  1.3 99.5 %shard_map.145 = (bf16[1,128,4096]{2,1,0:T(8,128)(2,1)}, f32[1,128]{1,0:T(1,128)}, bf16[1,1,1601,1024]{3,2,1,0:T(8,128)(2,1)}, bf16[1,128,4096]{2,1,0:T(8,128)(2...) custom-call(bf16[1,128,4096]{2,1,0:T(8,128)(2,1)} %xq.1, bf16[1,128,4096]{2,1,0:T(8,128)(2,1)} %xc.1, ...), custom_call_target="tpu_custom_call" | custom-call | flops 11827937280 | bytes 14680064 | tf_op jit(solution)/shard_map/pallas_call | solution.py:433
  100.8 0.0 copy-start
  100.8 7.4 %shard_map.146 = (bf16[1,128,4096]{2,1,0:T(8,128)(2,1)}, bf16[1,1,1601,1024]{3,2,1,0:T(8,128)(2,1)}, bf16[1,128,4096]{2,1,0:T(8,128)(2,1)}, bf16[1,128,512]{2,1,0:T(8,128)(2,1)}, bf16[1,128,512]{2,1,0:T(8,128)(2,1)}) custom-call(bf16[1,128,4096]{2,1,0:T(8,128)(2,1)} %get-tuple-element.17.refs_0_, bf16[1,1,1601,1024]{3,2,1,0:T(8,128)(2,1)} %get-tuple-element.18.refs_1_, ...), custom_call_target="tpu_custom_call" | custom-call | tf_op jit(solution)/shard_map/pallas_call | solution.py:500
  108.2 0.0 copy-done
  108.3 0.5 slice_bitcast_fusion
Async XLA Ops:
  100.8 7.4 %copy-start = (f32[1,128]{1,0:T(1,128)S(1)}, f32[1,128]{1,0:T(1,128)}, u32[]{:S(2)}) copy-start(f32[1,128]{1,0:T(1,128)} %get-tuple-element.23) | copy-start | bytes 1540

commit v3 on v2

--- a/solution.py
+++ b/solution.py
@@ -84,17 +84,18 @@
 
 def kernel(
     xq, xc, gate, vis, bmap, sq, sk, sv, sc, doc,
-    xdq, gsum, vgrad, sdq, kgrad, valgrad,
+    xdq_v, gsum, vgrad, sdq_v, kgrad, valgrad,
     recv, own, xq_v, xc_v, sq_v, sc_v, line, pair, dline, dpair,
     kp, vp, k_t, q_s, c_s, tq_s, do_s, scores, eb, ds, bias, r_keep, esum, across, down, along,
-    gown, gsend, garr, xdq_v, sdq_v, og, ag, bg, xs, xr, bs, br, as_, ar,
-    ld_sem, own_sem, out_sem, v_ss, v_rs, h_ss, h_rs, d_ss, d_rs, g_ss, g_rs, s_ss, s_rs, a_ss, a_rs, b_ss, b_rs, c_ss, c_rs,
+    gown, gsend, garr, og, ag, bg, xs, xr, bs, br, as_, ar,
+    ld_sem, own_sem, v_ss, v_rs, h_ss, h_rs, d_ss, d_rs, g_ss, g_rs, s_ss, s_rs, a_ss, a_rs, b_ss, b_rs, c_ss, c_rs,
 ):
     count = lax.axis_size("seq")
     me = lax.axis_index("seq")
     par = lax.rem(me, 2)
     next1, prev1 = lax.rem(me + 1, count), lax.rem(me + count - 1, count)
     next2, prev2 = lax.rem(me + 2, count), lax.rem(me + count - 2, count)
+    next4, prev4 = lax.rem(me + 4, count), lax.rem(me + count - 4, count)
     other = me + 1 - 2 * par
     bm = bmap[0, 0]
 
@@ -112,7 +113,7 @@
         (down, y, count // ROW, "seq", [lax.rem(me + i * ROW, count) for i in range(1, count // ROW)], b_ss, b_rs),
         (along, z, depth, "dp", [lax.rem(z + i, depth) for i in range(1, depth)], c_ss, c_rs),
     )
-    partners = [("seq", device) for device in (next1, prev1, next2, prev2)]
+    partners = [("seq", device) for device in (next1, prev1, next2, prev2, next4, prev4)]
     for _, _, _, axis, devices, _, _ in stages:
         partners += [(axis, device) for device in devices]
     barrier = pltpu.get_barrier_semaphore()
@@ -146,9 +147,9 @@
         remote(dline.at[0], dline.at[1], d_ss.at[0], d_rs.at[0], next2),
     ]
     relay = [
-        remote(line.at[1, 0], line.at[2, 0], h_ss.at[2], h_rs.at[2], next2),
-        remote(line.at[1, 1], line.at[2, 1], h_ss.at[3], h_rs.at[3], next2),
-        remote(dline.at[1], dline.at[2], d_ss.at[1], d_rs.at[1], next2),
+        remote(sk.at[0], line.at[2, 0], h_ss.at[2], h_rs.at[2], next4),
+        remote(sv.at[0], line.at[2, 1], h_ss.at[3], h_rs.at[3], next4),
+        remote(dline.at[0], dline.at[2], d_ss.at[1], d_rs.at[1], next4),
     ]
     share0 = [
         remote(line.at[par, 0], pair.at[0, 0], h_ss.at[4], h_rs.at[4], other),
@@ -162,22 +163,22 @@
     ]
     for i in (2, 0, 1):
         first[i].start()
+        relay[i].start()
+    for i, src in parts:
+        remote(src, recv.at[i], v_ss.at[i], v_rs.at[i], next1).start()
     loads[0].wait()
     loads[1].wait()
-    for i in (2, 0, 1):
+    for i in (2, 0):
         first[i].wait_recv()
-        relay[i].start()
         share0[i].start()
-    for i, src in parts:
-        remote(src, recv.at[i], v_ss.at[i], v_rs.at[i], next1).start()
     for i in (2, 0):
         relay[i].wait_recv()
         share1[i].start()
     for i in (2, 0):
         share0[i].wait_recv()
         share1[i].wait_recv()
-    for copy in loads[2:]:
-        copy.wait()
+    loads[2].wait()
+    loads[3].wait()
 
     mine = dline[0, 0:1, :].astype(F32)
     lanes = lax.broadcasted_iota(jnp.int32, (TOK, TOK), 1)
@@ -234,6 +235,11 @@
         r_keep[g, 0:1, :] = r
         scale_rows(r, sc_v, g, do_s)
         spread(g, 1, dot(eb_w[...], do_s[...], NN))
+
+        @pl.when(g == 0)
+        def _():
+            first[1].wait_recv()
+            share0[1].start()
 
         @pl.when(g == 1)
         def _():
@@ -263,11 +269,9 @@
     share1[1].wait_recv()
     lax.fori_loop(0, KVH, self_values, 0)
     swap = remote(xs, xr, s_ss.at[0], s_rs.at[0], other)
-    far = remote(bs, br, s_ss.at[1], s_rs.at[1], prev2)
+    far = remote(bs, br, s_ss.at[1], s_rs.at[1], prev4)
     near = remote(as_, ar, s_ss.at[2], s_rs.at[2], prev2)
     swap.start()
-    sdq_out = pltpu.make_async_copy(sdq_v, sdq.at[0], out_sem.at[0])
-    sdq_out.start()
 
     def grad_copy(i):
         return remote(gsend.at[i], garr.at[i], g_ss.at[i], g_rs.at[i], prev1)
@@ -291,11 +295,17 @@
             gsend[i, pl.ds(b, n), :] = (part * give).astype(BF)
         grad_copy(i).start()
 
-    def finish_part(i):
+    def done_part(h, half):
+        i = 2 * h + half
+        column = pl.ds(pl.multiple_of(half * KVW + h * HD, HD), HD)
         grad_copy(i).wait_recv()
         for b, n in ((0, 400), (400, 400), (800, 400), (1200, 400), (WHOLE, 1)):
             rows = pl.ds(b, n)
-            own[i, rows, :] = (gown[i, rows, :] + garr[i, rows, :].astype(F32)).astype(BF)
+            vgrad[rows, column] = (gown[i, rows, :] + garr[i, rows, :].astype(F32)).astype(BF)
+
+    def done_group(h):
+        done_part(h, 1)
+        done_part(h, 0)
 
     def stage_copy(number, i):
         buffer, place, size, axis, devices, send, arrive = stages[number]
@@ -317,19 +327,6 @@
             total = total + buffer[i, 0:1, :]
         return total
 
-    def part_out(h, half):
-        column = pl.ds(pl.multiple_of(half * KVW + h * HD, HD), HD)
-        i = 2 * h + half
-        return pltpu.make_async_copy(own.at[i], vgrad.at[0, 0, :, column], own_sem.at[i])
-
-    def done_part(h, half):
-        finish_part(2 * h + half)
-        part_out(h, half).start()
-
-    def done_group(h):
-        done_part(h, 1)
-        done_part(h, 0)
-
     e_scr, d_scr = scores.at[pl.ds(0, NK)], scores.at[pl.ds(NK, NK)]
 
     def cross_group(h, carry):
@@ -375,30 +372,25 @@
             for half in range(2):
                 x0, x1 = xr[0, half].astype(F32), xr[1, half].astype(F32)
                 og[half] = og[half] + even * x0
-                ag[half] = ag[half] + (odd * x0 + even * x1)
+                as_[half] = (ag[half] + (odd * x0 + even * x1)).astype(BF)
                 bs[half] = (bg[half] + odd * x1).astype(BF)
             far.start()
+            near.start()
 
         @pl.when(h >= 2)
         def _():
             done_group(h - 2)
 
-        @pl.when(h == 1)
-        def _():
-            far.wait()
-            for half in range(2):
-                as_[half] = (ag[half] + br[half].astype(F32)).astype(BF)
-            near.start()
-
         return carry
 
+    loads[4].wait()
+    loads[5].wait()
     lax.fori_loop(0, KVH, cross_group, 0)
-    xdq_out = pltpu.make_async_copy(xdq_v, xdq.at[0], out_sem.at[1])
-    xdq_out.start()
 
     near.wait()
+    far.wait()
     for half, out in enumerate((kgrad, valgrad)):
-        out[0] = (og[half] + ar[half].astype(F32)).astype(BF)
+        out[...] = (og[half] + (ar[half].astype(F32) + br[half].astype(F32))).astype(BF)
 
     stage_start(1, stage_end(0))
     done_part(KVH - 2, 1)
@@ -412,35 +404,31 @@
             stage_copy(number, i).wait_send()
     for h in range(KVH):
         for half in (1, 0):
-            part_out(h, half).wait()
             grad_copy(2 * h + half).wait_send()
     for i, src in parts:
         remote(src, recv.at[i], v_ss.at[i], v_rs.at[i], next1).wait_send()
     for copy in first + relay + share0 + share1:
         copy.wait_send()
-    sdq_out.wait()
-    xdq_out.wait()
 
 
 def fused(*operands):
     anywhere = pl.BlockSpec(memory_space=pl.ANY)
     vmem = pl.BlockSpec(memory_space=pltpu.VMEM)
     smem = pl.BlockSpec(memory_space=pltpu.SMEM)
-    wide = (1, TOK, HEADS * HD)
     shape = jax.ShapeDtypeStruct
     dma = pltpu.SemaphoreType.DMA
     vm = pltpu.VMEM
     return pl.pallas_call(
         kernel,
         in_specs=[anywhere, anywhere, smem, anywhere, smem, anywhere, anywhere, anywhere, anywhere, vmem],
-        out_specs=[anywhere, vmem, anywhere, anywhere, vmem, vmem],
+        out_specs=[vmem] * 6,
         out_shape=[
-            shape(wide, BF),
+            vm((TOK, HEADS * HD), BF),
             shape((1, TOK), F32),
-            shape((1, 1, VROWS, 2 * KVW), BF),
-            shape(wide, BF),
-            shape((1, TOK, KVW), BF),
-            shape((1, TOK, KVW), BF),
+            vm((VROWS, 2 * KVW), BF),
+            vm((TOK, HEADS * HD), BF),
+            vm((TOK, KVW), BF),
+            vm((TOK, KVW), BF),
         ],
         scratch_shapes=[
             vm((2 * KVH, VROWS, HD), BF),
@@ -462,13 +450,11 @@
             *[vm((8, 8, TOK), F32)] * 3,
             vm((2 * KVH, VROWS, HD), F32),
             *[vm((2 * KVH, VROWS, HD), BF)] * 2,
-            *[vm((TOK, HEADS * HD), BF)] * 2,
             *[vm((2, TOK, KVW), F32)] * 3,
             *[vm((2, 2, TOK, KVW), BF)] * 2,
             *[vm((2, TOK, KVW), BF)] * 4,
             dma((6,)),
             dma((2 * KVH,)),
-            dma((2,)),
             *[dma((2 * KVH,))] * 2,
             *[dma((8,))] * 2,
             *[dma((4,))] * 2,
@@ -477,32 +463,33 @@
             *[dma((8,))] * 6,
         ],
         compiler_params=pltpu.CompilerParams(
-            collective_id=0, has_side_effects=True, vmem_limit_bytes=60 * 2**20
+            collective_id=0, has_side_effects=True, vmem_limit_bytes=54 * 2**20
         ),
         cost_estimate=pl.CostEstimate(flops=2 * 5 * NQ * KVH * HD * (NK + WIN), bytes_accessed=14 * 2**20, transcendentals=0),
     )(*operands)
 
 
 def settle_kernel(*refs):
+    *refs, sem = refs
     half = len(refs) // 2
-    for src, dst in zip(refs[:half], refs[half:]):
-        dst[...] = src[...]
-
-
-def settle(xdq, vgrad, sdq, kgrad, valgrad):
-    steps = 8
-    rows = TOK // steps
-    wide = pl.BlockSpec((1, rows, HEADS * HD), lambda i: (0, i, 0))
-    image = pl.BlockSpec((1, 1, 208, 2 * KVW), lambda i: (0, 0, i, 0))
-    narrow = pl.BlockSpec((1, rows, KVW), lambda i: (0, i, 0))
-    arrays = (xdq, vgrad, sdq, kgrad, valgrad)
-    specs = [wide, image, wide, narrow, narrow]
+    copies = []
+    for i, (src, dst) in enumerate(zip(refs[:half], refs[half:])):
+        copies.append(pltpu.make_async_copy(src, dst.at[(0,) * (len(dst.shape) - 2)], sem.at[i]))
+    for copy in copies:
+        copy.start()
+    for copy in copies:
+        copy.wait()
+
+
+def settle(*arrays):
+    shapes = [(1,) * (2 if x.shape[0] == VROWS else 1) + x.shape for x in arrays]
     return pl.pallas_call(
         settle_kernel,
-        grid=(steps,),
-        in_specs=specs,
-        out_specs=specs,
-        out_shape=[jax.ShapeDtypeStruct(x.shape, x.dtype) for x in arrays],
+        in_specs=[pl.BlockSpec(memory_space=pltpu.VMEM)] * len(arrays),
+        out_specs=[pl.BlockSpec(memory_space=pl.ANY)] * len(arrays),
+        out_shape=[jax.ShapeDtypeStruct(x, BF) for x in shapes],
+        scratch_shapes=[pltpu.SemaphoreType.DMA((len(arrays),))],
+        compiler_params=pltpu.CompilerParams(vmem_limit_bytes=2**20),
     )(*arrays)
 
 

time: 109 us -> 103 us (0.945)
  Pallas kernels: 107 us -> 101 us
    pallas_call x1, Pallas kernels: 7.43 us -> 2.49 us  [settle(): pl.pallas_call(settle_kernel, in_specs=[pl.BlockSpec(memory_space=pltpu.V...]
    pallas_call x1, Pallas kernels: 99.5 us -> 98.4 us  [fused(): pl.pallas_call(kernel, in_specs=[anywhere, anywhere, smem, anywhere, smem...]
where the time goes in v3:
time: 103 us
  Pallas kernels  101 us (98%)
  between operations  1.31 us (1%)
    pallas_call x1, Pallas kernels, fused(): pl.pallas_call(kernel, in_specs=[anywhere, anywhere, smem, anywhere, smem...  98.4 us
    pallas_call x1, Pallas kernels, settle(): pl.pallas_call(settle_kernel, in_specs=[pl.BlockSpec(memory_space=pltpu.V...  2.49 us

profile of v3, /device:TPU:6, one launch (start us, length us, event | category | flops | bytes accessed | tf_op | source)
XLA Modules:
  0.0 102.7 jit_solution(6687404684770276620)
XLA Ops:
  1.3 98.4 %shard_map.145 = (bf16[128,4096]{1,0:T(8,128)(2,1)S(1)}, f32[1,128]{1,0:T(1,128)}, bf16[1601,1024]{1,0:T(8,128)(2,1)S(1)}, bf16[128,4096]{1,0:T(8,128)(2,1)S(1)}...) custom-call(bf16[1,128,4096]{2,1,0:T(8,128)(2,1)} %xq.1, bf16[1,128,4096]{2,1,0:T(8,128)(2,1)} %xc.1, ...), custom_call_target="tpu_custom_call" | custom-call | flops 11827937280 | bytes 14680064 | tf_op jit(solution)/shard_map/pallas_call | solution.py:421
  99.7 0.0 copy-start
  99.7 2.5 %shard_map.146 = (bf16[1,128,4096]{2,1,0:T(8,128)(2,1)}, bf16[1,1,1601,1024]{3,2,1,0:T(8,128)(2,1)}, bf16[1,128,4096]{2,1,0:T(8,128)(2,1)}, bf16[1,128,512]{2,1,0:T(8,128)(2,1)}, bf16[1,128,512]{2,1,0:T(8,128)(2,1)}) custom-call(bf16[128,4096]{1,0:T(8,128)(2,1)S(1)} %get-tuple-element.17.refs_0_, bf16[1601,1024]{1,0:T(8,128)(2,1)S(1)} %get-tuple-element.18.refs_1_, ...), custom_call_target="tpu_custom_call" | custom-call | tf_op jit(solution)/shard_map/pallas_call | solution.py:486
  102.2 0.0 copy-done
  102.2 0.5 slice_bitcast_fusion
Async XLA Ops:
  99.7 2.5 %copy-start = (f32[1,128]{1,0:T(1,128)S(1)}, f32[1,128]{1,0:T(1,128)}, u32[]{:S(2)}) copy-start(f32[1,128]{1,0:T(1,128)} %get-tuple-element.23) | copy-start | bytes 1540
